TPU v7x, 32 devices: a whole 2x2x4 slice. The times are simulated.
32 devices in a mesh: group: 4 (over z), tile: 8 (over y, x, core).
Axes of the slice: x: 2, y: 2, z: 4, core: 2. Of those that a mesh axis runs over, the one named last changes fastest.
Arguments:
- potential: float32 [64, 8192], P('group', 'tile'), may hold values from -6 to 6
- species_inputs: bfloat16 [7, 64, 8192], P(None, 'group', 'tile'), may hold values from -6 to 6
- diffusion: float32 [4, 8192], P(None, 'tile'), may hold values from 0.02 to 0.2
- neighbours: int32 [4, 8192], P(None, 'tile'), may hold values from 0 to 1535, as said below
- sunlit_column_index: int32 [4, 8, 256], P('group', 'tile'), may hold values from 0 to 255, each once within a row
- day_count: int32 [4, 8], P('group', 'tile'), may hold values from 0 to 256, as said below
- zenith: bfloat16 [4, 8, 256], P('group', 'tile'), may hold values from 0.099609375 to 1
- lw_first: bfloat16 [8, 64], replicated, may hold values from -2 to 2
- lw_bias: float32 [64], replicated, may hold values from -3 to 3
- lw_second: bfloat16 [64, 64], replicated, may hold values from -0.75 to 0.75
- lw_depth: bfloat16 [64, 256], replicated, may hold values from -0.75 to 0.75
- lw_fraction: bfloat16 [64, 256], replicated, may hold values from -0.75 to 0.75
- sw_first: bfloat16 [8, 64], replicated, may hold values from -2 to 2
- sw_bias: float32 [64], replicated, may hold values from -3 to 3
- sw_second: bfloat16 [64, 64], replicated, may hold values from -0.75 to 0.75
- sw_depth: bfloat16 [64, 224], replicated, may hold values from -0.75 to 0.75
- solar_flux: float32 [224], replicated, may hold values from 0.5 to 2
Outputs:
- evolved: float32 [64, 8192], P('group', 'tile')
Inputs may be any that keep to these rules, and one draw needn't show every extreme that they name: neighbours[k, c] - 256 - (c mod 1024) is a nonzero offset between -256 and 256. `sunlit_column_index`: each list [g, t, :] is a permutation of 0 .. 255. day_count[g, 2 i] + day_count[g, 2 i + 1] = 256 for every g and i.
All inputs are finite; a program needn't handle non-finite values.
Results may differ from a plain program's by a relative error of at most 0.0003.
Values may be sent and summed in bfloat16 or wider, within the bound.
No kernel may reach another device: no remote copies, remote signals or barrier semaphores. Data moves between devices by JAX's collectives and lax.ppermute only.
A program may use at most 128 MiB of HBM per device.

v0:
```python
import functools
import math

import jax
import jax.numpy as jnp
from jax import lax
from jax.experimental import pallas as pl
from jax.experimental.pallas import tpu as pltpu
from jax.sharding import PartitionSpec as P

HW = 256
LANES = 128
SUBS = 8

depth_scale = 0.1
heat_scale = 12.0
LOG2E = 1.4426950408889634
LN2 = 0.6931471805599453
SAFE = 120.0

F32 = jnp.float32
BF16 = jnp.bfloat16
VMEM = pl.BlockSpec(memory_space=pltpu.VMEM)
ANY = pl.BlockSpec(memory_space=pl.ANY)
HBM = pl.BlockSpec(memory_space=pltpu.HBM)
SMEM = pl.BlockSpec(memory_space=pltpu.SMEM)
PARAMS = pltpu.CompilerParams(vmem_limit_bytes=48 * 1024 * 1024)


def call(body, outs, ins, scratch=(), flops=0, trans=0, after=None, where=VMEM):
    in_specs = [SMEM if a.size == 1 else where for a in ins]
    if after is not None:
        whole, ins = body, [after, *ins]
        in_specs = [ANY, *in_specs]

        def body(_, *refs):
            whole(*refs)

    return pl.pallas_call(
        body,
        out_shape=outs,
        in_specs=in_specs,
        out_specs=[VMEM for _ in outs],
        scratch_shapes=list(scratch),
        compiler_params=PARAMS,
        cost_estimate=pl.CostEstimate(
            flops=flops,
            transcendentals=trans,
            bytes_accessed=sum(a.size * a.dtype.itemsize for a in list(ins) + list(outs)),
        ),
    )(*ins)


def shaped(shape, dtype):
    return jax.ShapeDtypeStruct(shape, dtype)


def iota(shape, dim):
    return lax.broadcasted_iota(jnp.int32, shape, dim)


def mm(a, b):
    return jnp.dot(a, b, preferred_element_type=F32)


def far_first(n):
    return [0, *range(n - 1, 0, -1)]


def partners(me, pieces):
    return [(me[0] ^ bit, piece) for bit, piece in zip(far_first(len(pieces)), pieces)]


def lane_take(x, idx):
    return jnp.take_along_axis(x, idx, axis=1, mode="promise_in_bounds")


def diffused(src, src_at, table, weight, within, at):
    reach = HW // LANES
    wide = 2 * reach + 1
    rows = src.shape[0]
    groups = range(0, rows, SUBS)
    base = at - src_at
    middle = [src[r : r + SUBS, base : base + LANES] for r in groups]
    total = [jnp.zeros_like(m) for m in middle]
    for k in range(table.shape[0]):
        place = jnp.broadcast_to(table[k : k + 1, within : within + LANES], (SUBS, LANES)) - within
        lane = place & (LANES - 1)
        which = place >> (LANES.bit_length() - 1)
        factor = jnp.broadcast_to(weight[k : k + 1, within : within + LANES], (SUBS, LANES))
        tests = [which == w for w in range(1, wide)]
        for n, r in enumerate(groups):
            near = None
            for w in range(wide):
                lo = base + (w - reach) * LANES
                got = lane_take(src[r : r + SUBS, lo : lo + LANES], lane)
                near = got if w == 0 else jnp.where(tests[w - 1], got, near)
            total[n] = total[n] + factor * (near - middle[n])
    return [(r, m, m + t) for r, m, t in zip(groups, middle, total)]


def pack_body(me, own, table, weight, species, out, *rest):
    pieces, (table_here, weight_here, sems) = rest[:-3], rest[-3:]
    slab = own.shape[0]
    near = table.shape[0]
    cols = pieces[0].shape[2]
    moves = [
        pltpu.make_async_copy(own, out.at[0:slab], sems.at[0]),
        pltpu.make_async_copy(table, table_here, sems.at[1]),
        pltpu.make_async_copy(weight, weight_here, sems.at[2]),
    ]
    for source, piece in partners(me, pieces):
        at = pl.ds(pl.multiple_of(source * cols, LANES), cols)
        moves.append(pltpu.make_async_copy(species.at[:, :, at], piece, sems.at[len(moves)]))
    for move in moves:
        move.start()
    for move in moves:
        move.wait()
    out[slab : slab + near, :] = table_here[...].astype(F32)
    out[slab + near :, :] = weight_here[...]


def sections_body(
    me, place, outer, inner, own, table, weight, third_out, *rest
):
    pieces, (frame, first, second, tables, weights) = rest[:-5], rest[-5:]
    slab, tile = own.shape
    near = table.shape[0]
    cols = tile // len(pieces)
    odd = place[0] & 1
    for side, packed in ((odd, outer), (1 - odd, inner)):
        at = pl.ds(pl.multiple_of(side * (2 * tile), LANES), tile)
        frame[:, at] = packed[0:slab, :]
        tables[side * 2] = packed[slab : slab + near, :].astype(jnp.int32)
        weights[side * 2] = packed[slab + near : slab + 2 * near, :]
    frame[:, tile : 2 * tile] = own[...]
    tables[1] = table[...]
    weights[1] = weight[...]

    def run(src, src_at, halo, put):
        for at in range(tile - halo, 2 * tile + halo, LANES):
            t = at // tile
            for r, _, value in diffused(src, src_at, tables.at[t], weights.at[t], at - t * tile, at):
                put(r, at, value)

    def put_first(r, at, value):
        first[r : r + SUBS, at : at + LANES] = value

    def put_second(r, at, value):
        start = frame[r : r + SUBS, at : at + LANES]
        second[r : r + SUBS, at : at + LANES] = 0.75 * start + 0.25 * value

    def put_third(r, at, value):
        start = frame[r : r + SUBS, at : at + LANES]
        lo = at - tile + HW
        third_out[r : r + SUBS, lo : lo + LANES] = start / 3.0 + (2.0 / 3.0) * value

    run(frame, 0, 3 * HW, put_first)
    run(first, 0, 2 * HW, put_second)
    run(second, 0, HW, put_third)
    for goal, out in partners(me, pieces):
        lo = pl.multiple_of(HW + goal * cols, LANES)
        out[...] = third_out[:, pl.ds(lo, cols)].astype(BF16)


def closing_body(third, table, weight, out):
    tile = out.shape[1]
    for at in range(0, tile, LANES):
        for r, _, value in diffused(third, -HW, table, weight, at, at):
            out[r : r + SUBS, at : at + LANES] = value


def turned_over(matrix):
    return matrix.astype(F32).T


def head_parts(weight, out, at):
    hid, gpts = weight.shape
    scaled = LOG2E * turned_over(weight[...])
    high = scaled.astype(BF16)
    out[at : at + gpts, 0:hid] = high
    out[at : at + gpts, hid:] = (scaled - high.astype(F32)).astype(BF16)


def reach_of(heads):
    sums = mm(jnp.abs(heads[...]), jnp.ones((heads.shape[1], LANES), BF16))
    return jnp.broadcast_to(jnp.max(sums, axis=0, keepdims=True), (2 * SUBS, LANES))


def prepare_body(
    count, listing, zenith, w1, b1, w2, wd, wf, v1, c1, v2, vd, flux,
    kept_out, sent_out, kept_cos, sent_cos, slot_of,
    w1_out, b1_out, w2_out, heads_out, reach_out, v1_out, c1_out, v2_out, vd_out, vreach_out, flux_out,
):
    for weight, out in ((w1, w1_out), (w2, w2_out), (v1, v1_out), (v2, v2_out)):
        out[...] = (0.5 * turned_over(weight[...])).astype(BF16)
    head_parts(wd, heads_out, 0)
    head_parts(wf, heads_out, wd.shape[1])
    head_parts(vd, vd_out, 0)
    reach_out[...] = reach_of(heads_out)
    vreach_out[...] = reach_of(vd_out)
    for row, out, scale in ((b1, b1_out, 0.5), (c1, c1_out, 0.5), (flux, flux_out, 1.0)):
        out[...] = scale * jnp.broadcast_to(row[...], (LANES, row.shape[1])).T
    cols = listing.shape[-1]
    half = cols // 2
    sunlit = count[0, 0]
    label = iota((cols, half), 0)
    slot = iota((cols, half), 1)
    first = jnp.broadcast_to(listing[0, :, 0:half], (cols, half)) == label
    last = jnp.broadcast_to(listing[0, :, half:cols], (cols, half)) == label
    kept = jnp.where(first & (slot < sunlit), 1.0, 0.0).astype(BF16)
    sent = jnp.where(last & (slot + half < sunlit), 1.0, 0.0).astype(BF16)
    kept_out[...] = kept
    sent_out[...] = sent
    cosine = jnp.broadcast_to(zenith[0].astype(F32), (2 * SUBS, cols)).astype(BF16)
    sent_cos[...] = mm(cosine, sent).astype(BF16)
    kept_cos[...] = mm(cosine, kept)[0:SUBS]
    hits = jnp.where(jnp.concatenate([first, last], axis=1), 1.0, 0.0).astype(BF16)
    numbers = iota((2 * SUBS, cols), 1).astype(F32).astype(BF16)
    found = lax.dot_general(numbers, hits, (((1,), (1,)), ((), ())), preferred_element_type=F32)
    slot_of[...] = found[0:SUBS].astype(jnp.int32)


def join_body(n_group, me, *rest):
    gases, warms = rest[:n_group], rest[n_group : 2 * n_group]
    kept, sent, sent_cos, packed, outgoing, kept_x, spread = rest[2 * n_group :]
    slab = warms[0].shape[0]
    for (source, gas), warm in zip(partners(me, gases), warms):
        for h in range(packed.shape[0]):
            at = slice(h * LANES, (h + 1) * LANES)
            spread[0:slab, :] = warm[:, at].astype(F32)
            for f in range(gas.shape[0]):
                spread[(f + 1) * slab : (f + 2) * slab, :] = gas[f, :, at].astype(F32)
            for l in range(slab):
                row = pl.multiple_of((source * slab + l) * SUBS, SUBS)
                packed[h, pl.ds(row, SUBS), :] = spread[pl.ds(l, SUBS, stride=slab), :]
    cells = packed.shape[1]
    first, last = packed[0].astype(BF16), packed[1].astype(BF16)
    outgoing[0:cells, :] = (mm(first, sent[0:LANES]) + mm(last, sent[LANES:])).astype(BF16)
    outgoing[cells:, :] = sent_cos[...]
    kept_x[...] = mm(first, kept[0:LANES]) + mm(last, kept[LANES:])


def softplus2(z):
    return lax.log2(1.0 + jnp.exp2(z))


def softplus2_guarded(z):
    return jnp.maximum(z, softplus2(jnp.minimum(z, SAFE)))


def silu_of_half(v):
    half = v.astype(BF16)
    return half + half * jnp.tanh(half)


def sweep(x, first, bias, second, heads, reach, start, gpts, rate, both, buffers, chunk_rows):
    ones, hids, zs, trans, parts, peak = buffers
    step_levels = zs.shape[2] // LANES
    one_a, one_b = ones.at[0], ones.at[1]
    hid_a, hid_b = hids.at[0], hids.at[1]
    z_a, z_b = zs.at[0], zs.at[1]
    levels = x.shape[0] // SUBS
    steps = levels // step_levels
    wide = step_levels * LANES
    rows = heads.shape[0]
    col_cut = 2 * LANES
    chunk = chunk_rows
    units = first.shape[0]
    unit_cut = units // 2

    def first_tasks(t, out):
        def task(r):
            row = jnp.minimum(t, steps - 1) * (step_levels * SUBS)
            tiles = [
                x[pl.ds(pl.multiple_of(row + i * SUBS, SUBS), SUBS), :] for i in range(step_levels)
            ]
            v = mm(first[r : r + unit_cut, :], jnp.concatenate(tiles, axis=1).astype(BF16))
            v = v + jnp.concatenate([bias[r : r + unit_cut, :]] * step_levels, axis=1)
            out[r : r + unit_cut, :] = silu_of_half(v)

        return [functools.partial(task, r) for r in range(0, units, unit_cut)]

    def second_tasks(one, out):
        def task(r):
            v = mm(second[r : r + unit_cut, :], one[...])
            value = silu_of_half(v)
            out[r : r + unit_cut, :] = value
            out[units + r : units + r + unit_cut, :] = value
            most = peak[...]
            for i in range(0, unit_cut, 2 * SUBS):
                for at in range(0, wide, LANES):
                    most = jnp.maximum(most, value[i : i + 2 * SUBS, at : at + LANES])
            peak[...] = most

        return [functools.partial(task, r) for r in range(0, units, unit_cut)]

    def optics_tasks(hid, out):
        def task(lo):
            at = slice(lo, lo + col_cut)
            out[:, at] = mm(heads[...], hid[:, at])

        return [functools.partial(task, lo) for lo in range(0, wide, col_cut)]

    def consume_tasks(z, total):
        def product(lo):
            return z[lo : lo + chunk, :]

        def task(lo):
            carry = trans[lo : lo + chunk, :]
            depth = product(lo)
            share = product(gpts + lo) if both else None
            for i in range(step_levels):
                at = slice(i * LANES, (i + 1) * LANES)
                following = carry * jnp.exp2(softplus2(depth[:, at]) * rate)
                term = following
                if both:
                    term = (carry - following) * softplus2(share[:, at])
                for r in range(0, chunk, SUBS):
                    part = term[r : r + SUBS]
                    total[i] = part if total[i] is None else total[i] + part
                carry = following
            trans[lo : lo + chunk, :] = carry

        return [functools.partial(task, lo) for lo in range(0, gpts, chunk)]

    def woven(main, side):
        done = 0
        for n, task in enumerate(main):
            while done < len(side) and done * len(main) <= n * len(side):
                side[done]()
                done += 1
            task()
        for task in side[done:]:
            task()

    def plain(tasks):
        for task in tasks:
            task()

    def run():
        trans[...] = start
        if not both:
            parts[0:SUBS, :] = jnp.sum(start.reshape(gpts // SUBS, SUBS, LANES), axis=0)

        def step(t, z, z_next, hid_next, hid_later, one_later, one_last):
            total = [None] * step_levels
            side = second_tasks(one_later, hid_later) + first_tasks(t + 3, one_last)
            woven(consume_tasks(z, total), optics_tasks(hid_next, z_next) + side)
            for i in range(step_levels):
                at = pl.multiple_of((t * step_levels + i + 1) * SUBS, SUBS)
                parts[pl.ds(at, SUBS), :] = total[i]

        def two(i, _):
            most = jnp.max(peak[...].astype(F32) * reach[...])
            step(2 * i, z_a, z_b, hid_b, hid_a, one_a, one_b)
            step(2 * i + 1, z_b, z_a, hid_a, hid_b, one_b, one_a)
            return most

        plain(first_tasks(0, one_a))
        plain(second_tasks(one_a, hid_a))
        plain(first_tasks(1, one_b))
        plain(optics_tasks(hid_a, z_a))
        plain(second_tasks(one_b, hid_b))
        plain(first_tasks(2, one_a))
        return lax.fori_loop(0, steps // 2, two, jnp.float32(0.0))

    def run_guarded():
        trans[...] = start
        at = slice(0, LANES)

        def level(l, _):
            tile = x[pl.ds(pl.multiple_of(l * SUBS, SUBS), SUBS), :].astype(BF16)
            hidden = silu_of_half(mm(first[...], tile) + bias[...])
            hidden = silu_of_half(mm(second[...], hidden))
            z_a[:, at] = mm(heads[...], jnp.concatenate([hidden, hidden], axis=0))

            def piece(c, total):
                lo = pl.multiple_of(c * SUBS, SUBS)
                carry = trans[pl.ds(lo, SUBS), :]
                depth = softplus2_guarded(z_a[pl.ds(lo, SUBS), at])
                following = carry * jnp.exp2(depth * rate)
                trans[pl.ds(lo, SUBS), :] = following
                if not both:
                    return total + following
                share = softplus2_guarded(z_a[pl.ds(pl.multiple_of(gpts + lo, SUBS), SUBS), at])
                return total + (carry - following) * share

            total = lax.fori_loop(0, gpts // SUBS, piece, jnp.zeros((SUBS, LANES), F32))
            parts[pl.ds(pl.multiple_of((l + 1) * SUBS, SUBS), SUBS), :] = total
            return 0

        lax.fori_loop(0, levels, level, 0)

    peak[...] = jnp.ones_like(peak)
    most = run()
    pl.when(most > SAFE)(run_guarded)
    emitted = None
    for s in range(SUBS):
        part = parts[pl.ds(s + SUBS, levels, stride=SUBS), :]
        if not both:
            part = parts[pl.ds(s, levels, stride=SUBS), :] - part
        emitted = part if emitted is None else emitted + part
    return emitted


def sweep_scratch(hid, rows, gpts, levels, step_levels=4):
    wide = step_levels * LANES
    return [
        pltpu.VMEM((2, hid, wide), BF16),
        pltpu.VMEM((2, 2 * hid, wide), BF16),
        pltpu.VMEM((2, rows, wide), F32),
        pltpu.VMEM((gpts, LANES), F32),
        pltpu.VMEM(((levels + 1) * SUBS, LANES), F32),
        pltpu.VMEM((2 * SUBS, LANES), BF16),
    ]


def longwave_body(which, packed, first, bias, second, heads, reach, out, *buffers):
    gpts = heads.shape[0] // 2
    levels = out.shape[0]
    x = packed.at[which]
    emitted = sweep(
        x, first, bias, second, heads, reach, jnp.ones((gpts, LANES), F32), gpts,
        -depth_scale, True, buffers, 2 * SUBS if which else SUBS,
    )
    planck = jnp.exp(0.25 * x[pl.ds(0, levels, stride=SUBS), :])
    out[...] = -(heat_scale * LN2 / gpts) * planck * emitted


def shortwave_body(
    count, kept_x, kept_cos, in_x, first, bias, second, heads, reach, flux, out, work_x, *buffers
):
    cells, half = kept_x.shape
    gpts = heads.shape[0]
    slot = iota((half, half), 1) - count[0, 0]
    placed = jnp.where(slot == iota((half, half), 0), 1.0, 0.0).astype(BF16)
    work_x[...] = kept_x[...] + mm(in_x[0:cells, :], placed)
    cosine = kept_cos[...] + mm(in_x[cells:, :], placed)[0:SUBS]
    cosine = jnp.where(cosine > 0.0, cosine, 1.0)
    emitted = sweep(
        work_x, first, bias, second, heads, reach, flux[...], gpts,
        -depth_scale / cosine, False, buffers, SUBS,
    )
    out[...] = (heat_scale / gpts) * cosine[0:1] * emitted


def finish_body(me, count, long_first, long_last, work, partner, slot_of, *rest):
    pieces, heat = rest[:-1], rest[-1]
    levels, cols = heat.shape
    half = cols // 2
    slab = pieces[0].shape[0]
    sunlit = count[0, 0]
    for lo, long in ((0, long_first), (half, long_last)):
        slot = slot_of[:, lo : lo + half]
        here = slot < half
        place = jnp.where(here, slot, slot + half - sunlit) & (half - 1)
        lit = slot < sunlit
        for r in range(0, levels, SUBS):
            near = lane_take(work[r : r + SUBS, :], place)
            far = lane_take(partner[r : r + SUBS, :], place)
            short = jnp.where(lit, jnp.where(here, near, far), 0.0)
            heat[r : r + SUBS, lo : lo + half] = long[r : r + SUBS, :] + short
    for goal, out in partners(me, pieces):
        out[...] = heat[pl.ds(pl.multiple_of(goal * slab, SUBS), slab), :]


def add_body(me, closed, *rest):
    pieces, out = rest[:-1], rest[-1]
    cols = pieces[0].shape[1]
    for source, piece in partners(me, pieces):
        at = pl.ds(pl.multiple_of(source * cols, LANES), cols)
        out[:, at] = closed[:, at] + piece[...]


def per_device(
    potential, species, diffusion, neighbours, listing, day_count, zenith,
    lw_first, lw_bias, lw_second, lw_depth, lw_fraction,
    sw_first, sw_bias, sw_second, sw_depth, solar_flux,
):
    n_group = lax.axis_size("group")
    n_tile = lax.axis_size("tile")
    assert n_group & (n_group - 1) == 0 and n_tile % 2 == 0
    me = lax.axis_index("group").astype(jnp.int32).reshape(1)
    place = lax.axis_index("tile").astype(jnp.int32).reshape(1)
    slab, tile = potential.shape
    gases = species.shape[0]
    cols = tile // n_group
    half = cols // 2
    levels = slab * n_group
    hid = lw_first.shape[1]
    lw_gpts = lw_depth.shape[1]
    sw_gpts = sw_depth.shape[1]

    def outward(value):
        across = [(i, (i + 1 if i % 2 else i - 1) % n_tile) for i in range(n_tile)]
        return lax.ppermute(value, "tile", across)

    def paired(value):
        return lax.ppermute(value, "tile", [(i, i ^ 1) for i in range(n_tile)])

    def swapped(value, bit):
        return lax.ppermute(value, "group", [(i, i ^ bit) for i in range(n_group)])

    def exchanged(pieces):
        return [swapped(p, bit) if bit else p for bit, p in zip(far_first(n_group), pieces)]

    near = neighbours.shape[0]
    raw = (potential, neighbours, diffusion, species)
    framing, *gas_cuts = call(
        pack_body,
        [shaped((slab + 2 * near, tile), F32)] + [shaped((gases, slab, cols), BF16)] * n_group,
        [me, *(pltpu.with_memory_space_constraint(a, pltpu.HBM) for a in raw)],
        [
            pltpu.VMEM(neighbours.shape, jnp.int32),
            pltpu.VMEM(diffusion.shape, F32),
            pltpu.SemaphoreType.DMA((3 + n_group,)),
        ],
        where=HBM,
    )
    inner = paired(framing)
    outer = outward(framing)
    gas_pieces = exchanged(gas_cuts)

    (
        kept, sent, kept_cos, sent_cos, slot_of,
        lw_one, lw_shift, lw_two, lw_heads, lw_reach,
        sw_one, sw_shift, sw_two, sw_heads, sw_reach, flux,
    ) = call(
        prepare_body,
        [
            shaped((cols, half), BF16),
            shaped((cols, half), BF16),
            shaped((SUBS, half), F32),
            shaped((2 * SUBS, half), BF16),
            shaped((SUBS, cols), jnp.int32),
            shaped(lw_first.shape[::-1], BF16),
            shaped((hid, LANES), F32),
            shaped(lw_second.shape[::-1], BF16),
            shaped((2 * lw_gpts, 2 * hid), BF16),
            shaped((2 * SUBS, LANES), F32),
            shaped(sw_first.shape[::-1], BF16),
            shaped((hid, LANES), F32),
            shaped(sw_second.shape[::-1], BF16),
            shaped((sw_gpts, 2 * hid), BF16),
            shaped((2 * SUBS, LANES), F32),
            shaped((sw_gpts, LANES), F32),
        ],
        [
            day_count, listing, zenith,
            lw_first, lw_bias[None], lw_second, lw_depth, lw_fraction,
            sw_first, sw_bias[None], sw_second, sw_depth, solar_flux[None],
        ],
        after=framing,
    )

    third, *warm_cuts = call(
        sections_body,
        [shaped((slab, tile + 2 * HW), F32)] + [shaped((slab, cols), BF16)] * n_group,
        [me, place, outer, inner, potential, neighbours, diffusion],
        [pltpu.VMEM((slab, 3 * tile), F32)] * 3
        + [pltpu.VMEM((3, *neighbours.shape), jnp.int32), pltpu.VMEM((3, *diffusion.shape), F32)],
        flops=10_000_000,
    )
    warm_pieces = exchanged(warm_cuts)
    (closed,) = call(
        closing_body, [shaped((slab, tile), F32)], [third, neighbours, diffusion], flops=2_000_000
    )

    cells = levels * SUBS
    packed, out_x, kept_x = call(
        functools.partial(join_body, n_group),
        [
            shaped((cols // LANES, cells, LANES), F32),
            shaped((cells + 2 * SUBS, half), BF16),
            shaped((cells, half), F32),
        ],
        [me, *gas_pieces, *warm_pieces, kept, sent, sent_cos],
        [pltpu.VMEM((SUBS * slab, LANES), F32)],
    )
    in_x = paired(out_x)

    def longwave(which):
        (heat,) = call(
            functools.partial(longwave_body, which),
            [shaped((levels, half), F32)],
            [packed, lw_one, lw_shift, lw_two, lw_heads, lw_reach],
            sweep_scratch(hid, 2 * lw_gpts, lw_gpts, levels, 8),
            flops=4 * levels * half * hid * lw_gpts,
            trans=5 * levels * half * lw_gpts,
            after=work if which else None,
        )
        return heat

    long_first = longwave(0)
    (work,) = call(
        shortwave_body,
        [shaped((levels, half), F32)],
        [day_count, kept_x, kept_cos, in_x, sw_one, sw_shift, sw_two, sw_heads, sw_reach, flux],
        [pltpu.VMEM((cells, half), F32)] + sweep_scratch(hid, sw_gpts, sw_gpts, levels),
        flops=2 * levels * half * hid * sw_gpts,
        trans=3 * levels * half * sw_gpts,
        after=long_first,
    )
    partner = paired(work)
    long_last = longwave(1)
    heat_cuts = call(
        finish_body,
        [shaped((slab, cols), F32)] * n_group,
        [me, day_count, long_first, long_last, work, partner, slot_of],
        [pltpu.VMEM((levels, cols), F32)],
    )
    heat_pieces = exchanged(heat_cuts)
    (evolved,) = call(add_body, [shaped((slab, tile), F32)], [me, closed, *heat_pieces])
    return evolved


def solution(mesh):
    return jax.shard_map(
        per_device,
        mesh=mesh,
        in_specs=(
            P("group", "tile"),
            P(None, "group", "tile"),
            P(None, "tile"),
            P(None, "tile"),
            P("group", "tile", None),
            P("group", "tile"),
            P("group", "tile", None),
            *([P()] * 10),
        ),
        out_specs=P("group", "tile"),
        check_vma=False,
    )
```

profile of v0, /device:TPU:4, one launch (start us, length us, event | category | flops | bytes accessed | tf_op | source)
XLA Modules:
  0.0 289.7 jit_solution(15358044451404064423)
XLA Ops:
  0.0 1.1 shard_map.163
  1.1 0.1 collective-permute-start.1
  1.2 1.5 collective-permute-start
  2.7 3.6 %collective-permute-start.2 = (bf16[7,16,256]{2,1,0:T(8,128)(2,1)S(1)}, bf16[7,16,256]{2,1,0:T(8,128)(2,1)S(1)}, u32[]{:S(2)}, u32[]{:S(2)}) collective-permute-start(bf16[7,16,256]{2,1,0:T(8,128)(2,1)S(1)} %get-tuple-element.41), channel_id=1, source_target_pairs={{0,24},{8,16},{16,8},{24,0},{1,25},{9,17},{17,9},{25,1},{2,26},{10... | collective-permute-start | bytes 172040 | tf_op jit(solution)/shard_map/ppermute | solution.py:503
  6.3 0.0 collective-permute-start.3
  6.3 0.8 collective-permute-start.4
  7.1 0.0 collective-permute-done.1.inner
  7.1 0.0 collective-permute-done.outer
  7.1 0.0 copy-start.3
  7.1 0.0 copy-start.4
  7.1 0.0 copy-start.5
  7.2 0.0 copy-start.6
  7.2 0.0 copy-start.7
  7.2 2.7 shard_map.164
  9.9 3.7 %collective-permute-start.5 = (bf16[16,256]{1,0:T(8,128)(2,1)S(1)}, bf16[16,256]{1,0:T(8,128)(2,1)S(1)}, u32[]{:S(2)}, u32[]{:S(2)}) collective-permute-start(bf16[16,256]{1,0:T(8,128)(2,1)S(1)} %get-tuple-element.45), channel_id=1, source_target_pairs={{0,24},{8,16},{16,8},{24,0},{1,25},{9,17},{17,9},{25,1},{2,26},{10... | collective-permute-start | bytes 24584 | tf_op jit(solution)/shard_map/ppermute | solution.py:503
  13.6 0.0 collective-permute-start.6
  13.6 0.0 collective-permute-done.2.rest_1_
  13.6 0.0 copy-start.12
  13.6 0.0 copy-start.14
  13.6 0.8 collective-permute-start.7
  15.1 0.0 copy-start.9
  15.1 0.0 copy-start.8
  15.1 0.0 copy-start.10
  15.2 0.0 copy-start.13
  15.2 0.6 copy-done.9
  15.8 0.0 copy-done.8
  15.8 0.0 copy-done.10
  15.8 0.5 shard_map.166
  16.3 0.0 collective-permute-done.3.rest_2_
  16.3 0.0 collective-permute-done.4.rest_3_
  16.3 0.0 collective-permute-done.5.rest_5_
  16.3 1.8 collective-permute-done.6.rest_6_
  18.2 0.0 collective-permute-done.7.rest_7_
  18.2 0.5 shard_map.167
  18.6 0.1 collective-permute-start.8
  18.7 8.6 %shard_map.168._.long_first = f32[64,128]{1,0:T(8,128)S(1)} custom-call(f32[2,512,128]{2,1,0:T(8,128)S(1)} %get-tuple-element.51.packed.refs_0_, bf16[64,8]{1,0:T(8,128)(2,1)S(1)} %get-tuple-element.52.first.refs_1_, f32[64,128]{1,0:T(8,128)S(1)} %get-tuple-element.53.bias.refs_2_, bf16[64,64]{1,0:T(8,128)(2,1)S(1)} %get-tuple-element.54.second.refs_3_, ...), custom_call_target="tpu_custom_call" | custom-call | flops 536870912 | bytes 738304 | tf_op jit(solution)/shard_map/pallas_call | solution.py:39
  27.3 0.0 collective-permute-done.8.refs_3_
  27.3 79.1 %shard_map.169._.work = f32[64,128]{1,0:T(8,128)S(1)} custom-call(f32[64,128]{1,0:T(8,128)S(1)} %shard_map.168._.long_first, s32[1,1]{1,0:T(1,128)S(6)} %copy.18.refs_0_.count, f32[512,128]{1,0:T(8,128)S(1)} %get-tuple-element.57.refs_1_, f32[8,128]{1,0:T(8,128)S(1)} %get-tuple-element.58.refs_2_, bf16[528,128]{1,0:T(8,128)(2,1)S(1)} %collective-permute-done.8.refs_3_, ...), custom_call_target="tpu_custom_call" | custom-call | flops 234881024 | bytes 689156 | tf_op jit(solution)/shard_map/pallas_call | solution.py:39
  106.4 0.1 collective-permute-start.9
  106.5 8.6 %shard_map.170.long_last = f32[64,128]{1,0:T(8,128)S(1)} custom-call(f32[64,128]{1,0:T(8,128)S(1)} %shard_map.169._.work, f32[2,512,128]{2,1,0:T(8,128)S(1)} %get-tuple-element.51.packed.refs_0_, bf16[64,8]{1,0:T(8,128)(2,1)S(1)} %get-tuple-element.52.first.refs_1_, f32[64,128]{1,0:T(8,128)S(1)} %get-tuple-element.53.bias.refs_2_, ...), custom_call_target="tpu_custom_call" | custom-call | flops 536870912 | bytes 771072 | tf_op jit(solution)/shard_map/pallas_call | solution.py:39
  115.1 0.1 shard_map.171
  115.2 0.1 collective-permute-start.10
  115.3 170.1 %collective-permute-start.11 = (f32[16,256]{1,0:T(8,128)S(1)}, f32[16,256]{1,0:T(8,128)S(1)}, u32[]{:S(2)}, u32[]{:S(2)}) collective-permute-start(f32[16,256]{1,0:T(8,128)S(1)} %get-tuple-element.69), channel_id=1, source_target_pairs={{0,16},{8,24},{16,0},{24,8},{1,17},{9,25},{17,1},{25,9},{2,18},{10... | collective-permute-start | bytes 49160 | tf_op jit(solution)/shard_map/ppermute | solution.py:503
  285.4 0.0 collective-permute-start.12
  285.4 0.5 shard_map.165.closed
  285.9 1.4 collective-permute-done.11.rest_2_
  287.2 1.9 collective-permute-done.12.rest_3_
  289.1 0.6 shard_map.172
  (18 shorter events, 0.0 us)
Async XLA Ops:
  0.0 7.1 %copy-start = (f32[16,1024]{1,0:T(8,128)S(1)}, f32[16,1024]{1,0:T(8,128)}, u32[]{:S(2)}) copy-start(f32[16,1024]{1,0:T(8,128)} %own.3) | copy-start | bytes 196612
  0.0 7.1 %copy-start.1 = (s32[4,1024]{1,0:T(4,128)S(1)}, s32[4,1024]{1,0:T(4,128)}, u32[]{:S(2)}) copy-start(s32[4,1024]{1,0:T(4,128)} %table.5) | copy-start | bytes 49156
  0.0 7.1 %copy-start.2 = (f32[4,1024]{1,0:T(4,128)S(1)}, f32[4,1024]{1,0:T(4,128)}, u32[]{:S(2)}) copy-start(f32[4,1024]{1,0:T(4,128)} %weight.5) | copy-start | bytes 49156
  1.1 6.0 %collective-permute-start.1 = (f32[24,1024]{1,0:T(8,128)S(1)}, f32[24,1024]{1,0:T(8,128)S(1)}, u32[]{:S(2)}, u32[]{:S(2)}) collective-permute-start(f32[24,1024]{1,0:T(8,128)S(1)} %get-tuple-element.38._), channel_id=1, source_target_pairs={{0,1},{1,0},{2,3},{3,2},{4,5},{5,4},{6,7},{7,6},{8,9},{9,8},{10,11... | collective-permute-start | bytes 294920 | tf_op jit(solution)/shard_map/ppermute | solution.py:500
  1.2 5.9 %collective-permute-start = (f32[24,1024]{1,0:T(8,128)S(1)}, f32[24,1024]{1,0:T(8,128)S(1)}, u32[]{:S(2)}, u32[]{:S(2)}) collective-permute-start(f32[24,1024]{1,0:T(8,128)S(1)} %get-tuple-element.38._), channel_id=1, source_target_pairs={{0,7},{1,2},{2,1},{3,4},{4,3},{5,6},{6,5},{7,0},{8,15},{9,10},{10,... | collective-permute-start | bytes 294920 | tf_op jit(solution)/shard_map/ppermute | solution.py:497
  2.7 10.9 %collective-permute-start.2 = (bf16[7,16,256]{2,1,0:T(8,128)(2,1)S(1)}, bf16[7,16,256]{2,1,0:T(8,128)(2,1)S(1)}, u32[]{:S(2)}, u32[]{:S(2)}) collective-permute-start(bf16[7,16,256]{2,1,0:T(8,128)(2,1)S(1)} %get-tuple-element.41), channel_id=1, source_target_pairs={{0,24},{8,16},{16,8},{24,0},{1,25},{9,17},{17,9},{25,1},{2,26},{10... | collective-permute-start | bytes 172040 | tf_op jit(solution)/shard_map/ppermute | solution.py:503
  6.3 10.0 %collective-permute-start.3 = (bf16[7,16,256]{2,1,0:T(8,128)(2,1)S(1)}, bf16[7,16,256]{2,1,0:T(8,128)(2,1)S(1)}, u32[]{:S(2)}, u32[]{:S(2)}) collective-permute-start(bf16[7,16,256]{2,1,0:T(8,128)(2,1)S(1)} %get-tuple-element.42), channel_id=1, source_target_pairs={{0,16},{8,24},{16,0},{24,8},{1,17},{9,25},{17,1},{25,9},{2,18},{10... | collective-permute-start | bytes 172040 | tf_op jit(solution)/shard_map/ppermute | solution.py:503
  6.3 10.0 %collective-permute-start.4 = (bf16[7,16,256]{2,1,0:T(8,128)(2,1)S(1)}, bf16[7,16,256]{2,1,0:T(8,128)(2,1)S(1)}, u32[]{:S(2)}, u32[]{:S(2)}) collective-permute-start(bf16[7,16,256]{2,1,0:T(8,128)(2,1)S(1)} %get-tuple-element.43), channel_id=1, source_target_pairs={{0,8},{8,0},{16,24},{24,16},{1,9},{9,1},{17,25},{25,17},{2,10},{10... | collective-permute-start | bytes 172040 | tf_op jit(solution)/shard_map/ppermute | solution.py:503
  7.1 8.0 %copy-start.3 = (bf16[64,256]{1,0:T(8,128)(2,1)S(1)}, bf16[64,256]{1,0:T(8,128)(2,1)}, u32[]{:S(2)}) copy-start(bf16[64,256]{1,0:T(8,128)(2,1)} %refs_6_.1) | copy-start | bytes 98308
  7.1 8.0 %copy-start.4 = (bf16[64,256]{1,0:T(8,128)(2,1)S(1)}, bf16[64,256]{1,0:T(8,128)(2,1)}, u32[]{:S(2)}) copy-start(bf16[64,256]{1,0:T(8,128)(2,1)} %refs_7_.1) | copy-start | bytes 98308
  7.1 8.0 %copy-start.5 = (bf16[64,224]{1,0:T(8,128)(2,1)S(1)}, bf16[64,224]{1,0:T(8,128)(2,1)}, u32[]{:S(2)}) copy-start(bf16[64,224]{1,0:T(8,128)(2,1)} %refs_11_.1) | copy-start | bytes 86020
  7.2 8.0 %copy-start.6 = (bf16[64,64]{1,0:T(8,128)(2,1)S(1)}, bf16[64,64]{1,0:T(8,128)(2,1)}, u32[]{:S(2)}) copy-start(bf16[64,64]{1,0:T(8,128)(2,1)} %refs_5_.1) | copy-start | bytes 24580
  7.2 8.0 %copy-start.7 = (bf16[64,64]{1,0:T(8,128)(2,1)S(1)}, bf16[64,64]{1,0:T(8,128)(2,1)}, u32[]{:S(2)}) copy-start(bf16[64,64]{1,0:T(8,128)(2,1)} %refs_10_.1) | copy-start | bytes 24580
  9.9 6.4 %collective-permute-start.5 = (bf16[16,256]{1,0:T(8,128)(2,1)S(1)}, bf16[16,256]{1,0:T(8,128)(2,1)S(1)}, u32[]{:S(2)}, u32[]{:S(2)}) collective-permute-start(bf16[16,256]{1,0:T(8,128)(2,1)S(1)} %get-tuple-element.45), channel_id=1, source_target_pairs={{0,24},{8,16},{16,8},{24,0},{1,25},{9,17},{17,9},{25,1},{2,26},{10... | collective-permute-start | bytes 24584 | tf_op jit(solution)/shard_map/ppermute | solution.py:503
  13.6 4.5 %collective-permute-start.6 = (bf16[16,256]{1,0:T(8,128)(2,1)S(1)}, bf16[16,256]{1,0:T(8,128)(2,1)S(1)}, u32[]{:S(2)}, u32[]{:S(2)}) collective-permute-start(bf16[16,256]{1,0:T(8,128)(2,1)S(1)} %get-tuple-element.46), channel_id=1, source_target_pairs={{0,16},{8,24},{16,0},{24,8},{1,17},{9,25},{17,1},{25,9},{2,18},{10... | collective-permute-start | bytes 24584 | tf_op jit(solution)/shard_map/ppermute | solution.py:503
  13.6 1.6 copy-start.11
  13.6 1.6 copy-start.12
  13.6 1.6 copy-start.14
  13.6 4.5 %collective-permute-start.7 = (bf16[16,256]{1,0:T(8,128)(2,1)S(1)}, bf16[16,256]{1,0:T(8,128)(2,1)S(1)}, u32[]{:S(2)}, u32[]{:S(2)}) collective-permute-start(bf16[16,256]{1,0:T(8,128)(2,1)S(1)} %get-tuple-element.47), channel_id=1, source_target_pairs={{0,8},{8,0},{16,24},{24,16},{1,9},{9,1},{17,25},{25,17},{2,10},{10... | collective-permute-start | bytes 24584 | tf_op jit(solution)/shard_map/ppermute | solution.py:503
  15.1 0.7 copy-start.9
  15.1 0.7 copy-start.8
  15.1 0.7 copy-start.10
  15.2 0.7 copy-start.13
  18.6 8.7 %collective-permute-start.8 = (bf16[528,128]{1,0:T(8,128)(2,1)S(1)}, bf16[528,128]{1,0:T(8,128)(2,1)S(1)}, u32[]{:S(2)}, u32[]{:S(2)}) collective-permute-start(bf16[528,128]{1,0:T(8,128)(2,1)S(1)} %get-tuple-element.59), channel_id=1, source_target_pairs={{0,1},{1,0},{2,3},{3,2},{4,5},{5,4},{6,7},{7,6},{8,9},{9,8},{10,11... | collective-permute-start | bytes 405512 | tf_op jit(solution)/shard_map/ppermute | solution.py:500
  106.4 8.7 %collective-permute-start.9 = (f32[64,128]{1,0:T(8,128)S(1)}, f32[64,128]{1,0:T(8,128)S(1)}, u32[]{:S(2)}, u32[]{:S(2)}) collective-permute-start(f32[64,128]{1,0:T(8,128)S(1)} %shard_map.169._.work), channel_id=1, source_target_pairs={{0,1},{1,0},{2,3},{3,2},{4,5},{5,4},{6,7},{7,6},{8,9},{9,8},{10,11... | collective-permute-start | bytes 98312 | tf_op jit(solution)/shard_map/ppermute | solution.py:500
  115.2 170.7 %collective-permute-start.10 = (f32[16,256]{1,0:T(8,128)S(1)}, f32[16,256]{1,0:T(8,128)S(1)}, u32[]{:S(2)}, u32[]{:S(2)}) collective-permute-start(f32[16,256]{1,0:T(8,128)S(1)} %get-tuple-element.68), channel_id=1, source_target_pairs={{0,24},{8,16},{16,8},{24,0},{1,25},{9,17},{17,9},{25,1},{2,26},{10... | collective-permute-start | bytes 49160 | tf_op jit(solution)/shard_map/ppermute | solution.py:503
  115.3 172.0 %collective-permute-start.11 = (f32[16,256]{1,0:T(8,128)S(1)}, f32[16,256]{1,0:T(8,128)S(1)}, u32[]{:S(2)}, u32[]{:S(2)}) collective-permute-start(f32[16,256]{1,0:T(8,128)S(1)} %get-tuple-element.69), channel_id=1, source_target_pairs={{0,16},{8,24},{16,0},{24,8},{1,17},{9,25},{17,1},{25,9},{2,18},{10... | collective-permute-start | bytes 49160 | tf_op jit(solution)/shard_map/ppermute | solution.py:503
  285.4 3.7 %collective-permute-start.12 = (f32[16,256]{1,0:T(8,128)S(1)}, f32[16,256]{1,0:T(8,128)S(1)}, u32[]{:S(2)}, u32[]{:S(2)}) collective-permute-start(f32[16,256]{1,0:T(8,128)S(1)} %get-tuple-element.70), channel_id=1, source_target_pairs={{0,8},{8,0},{16,24},{24,16},{1,9},{9,1},{17,25},{25,17},{2,10},{10... | collective-permute-start | bytes 49160 | tf_op jit(solution)/shard_map/ppermute | solution.py:503
where the time goes:
time: 292 us; the launch traced here: 290 us
  starting transfers between devices  181 us (62%)
  Pallas kernels  102 us (35%)
  waiting for transfers between devices  5.05 us (2%)
    ppermute x9, starting transfers between devices, swapped(): return lax.ppermute(value, 'group', [(i, i ^ bit) for i in range(n_group)])  179 us
    pallas_call x10, Pallas kernels, call(): pl.pallas_call(body, out_shape=outs, in_specs=in_specs, out_specs=[VMEM f...  102 us
  transfers between devices with their start and end apart: 13, of which 3 were waited for; matrix products, arithmetic and copies ran while one was open for 0% of the time, Pallas kernels for 7%

commit v1 on v0

--- a/solution.py
+++ b/solution.py
@@ -63,12 +63,32 @@
     return jnp.dot(a, b, preferred_element_type=F32)
 
 
-def far_first(n):
-    return [0, *range(n - 1, 0, -1)]
-
-
-def partners(me, pieces):
-    return [(me[0] ^ bit, piece) for bit, piece in zip(far_first(len(pieces)), pieces)]
+def rounds(n):
+    if n == 4:
+        return [
+            {1: 2, 2: 1},
+            {2: 0, 1: 3},
+            {0: 3, 3: 0},
+            {3: 2, 0: 1},
+            {3: 1, 1: 0, 0: 2, 2: 3},
+        ]
+    return [{i: (i + by) % n for i in range(n)} for by in range(1, n)]
+
+
+def looked_up(me, table, n):
+    value = jnp.int32(-1)
+    for i in range(n):
+        value = jnp.where(me == i, jnp.int32(table.get(i, -1)), value)
+    return value
+
+
+def goals(me, n):
+    found = [looked_up(me[0], table, n) for table in rounds(n)]
+    return [me[0], *(jnp.where(f < 0, me[0], f) for f in found)]
+
+
+def origins(me, n):
+    return [me[0], *(looked_up(me[0], {g: s for s, g in t.items()}, n) for t in rounds(n))]
 
 
 def lane_take(x, idx):
@@ -99,7 +119,7 @@
     return [(r, m, m + t) for r, m, t in zip(groups, middle, total)]
 
 
-def pack_body(me, own, table, weight, species, out, *rest):
+def pack_body(n_group, me, own, table, weight, species, out, *rest):
     pieces, (table_here, weight_here, sems) = rest[:-3], rest[-3:]
     slab = own.shape[0]
     near = table.shape[0]
@@ -109,8 +129,8 @@
         pltpu.make_async_copy(table, table_here, sems.at[1]),
         pltpu.make_async_copy(weight, weight_here, sems.at[2]),
     ]
-    for source, piece in partners(me, pieces):
-        at = pl.ds(pl.multiple_of(source * cols, LANES), cols)
+    for goal, piece in zip(goals(me, n_group), pieces):
+        at = pl.ds(pl.multiple_of(goal * cols, LANES), cols)
         moves.append(pltpu.make_async_copy(species.at[:, :, at], piece, sems.at[len(moves)]))
     for move in moves:
         move.start()
@@ -121,12 +141,12 @@
 
 
 def sections_body(
-    me, place, outer, inner, own, table, weight, third_out, *rest
+    n_group, me, place, outer, inner, own, table, weight, third_out, *rest
 ):
     pieces, (frame, first, second, tables, weights) = rest[:-5], rest[-5:]
     slab, tile = own.shape
     near = table.shape[0]
-    cols = tile // len(pieces)
+    cols = tile // n_group
     odd = place[0] & 1
     for side, packed in ((odd, outer), (1 - odd, inner)):
         at = pl.ds(pl.multiple_of(side * (2 * tile), LANES), tile)
@@ -158,7 +178,7 @@
     run(frame, 0, 3 * HW, put_first)
     run(first, 0, 2 * HW, put_second)
     run(second, 0, HW, put_third)
-    for goal, out in partners(me, pieces):
+    for goal, out in zip(goals(me, n_group), pieces):
         lo = pl.multiple_of(HW + goal * cols, LANES)
         out[...] = third_out[:, pl.ds(lo, cols)].astype(BF16)
 
@@ -222,10 +242,11 @@
 
 
 def join_body(n_group, me, *rest):
-    gases, warms = rest[:n_group], rest[n_group : 2 * n_group]
-    kept, sent, sent_cos, packed, outgoing, kept_x, spread = rest[2 * n_group :]
+    kept, sent, sent_cos, packed, outgoing, kept_x, spread = rest[-7:]
+    count = (len(rest) - 7) // 2
+    gases, warms = rest[:count], rest[count : 2 * count]
     slab = warms[0].shape[0]
-    for (source, gas), warm in zip(partners(me, gases), warms):
+    def place(source, gas, warm):
         for h in range(packed.shape[0]):
             at = slice(h * LANES, (h + 1) * LANES)
             spread[0:slab, :] = warm[:, at].astype(F32)
@@ -234,6 +255,9 @@
             for l in range(slab):
                 row = pl.multiple_of((source * slab + l) * SUBS, SUBS)
                 packed[h, pl.ds(row, SUBS), :] = spread[pl.ds(l, SUBS, stride=slab), :]
+
+    for source, gas, warm in zip(origins(me, n_group), gases, warms):
+        pl.when(source >= 0)(functools.partial(place, jnp.maximum(source, 0), gas, warm))
     cells = packed.shape[1]
     first, last = packed[0].astype(BF16), packed[1].astype(BF16)
     outgoing[0:cells, :] = (mm(first, sent[0:LANES]) + mm(last, sent[LANES:])).astype(BF16)
@@ -249,12 +273,23 @@
     return jnp.maximum(z, softplus2(jnp.minimum(z, SAFE)))
 
 
+def power(y):
+    value = 1.0
+    terms = [LN2**k / math.factorial(k) for k in range(7)]
+    value = terms[6]
+    for term in terms[5::-1]:
+        value = value * y + term
+    for _ in range(4):
+        value = value * value
+    return value
+
+
 def silu_of_half(v):
     half = v.astype(BF16)
     return half + half * jnp.tanh(half)
 
 
-def sweep(x, first, bias, second, heads, reach, start, gpts, rate, both, buffers, chunk_rows):
+def sweep(x, first, bias, second, heads, reach, start, gpts, rate, both, buffers, form):
     ones, hids, zs, trans, parts, peak = buffers
     step_levels = zs.shape[2] // LANES
     one_a, one_b = ones.at[0], ones.at[1]
@@ -265,9 +300,9 @@
     wide = step_levels * LANES
     rows = heads.shape[0]
     col_cut = 2 * LANES
-    chunk = chunk_rows
+    chunk = SUBS
     units = first.shape[0]
-    unit_cut = units // 2
+    unit_cut = units
 
     def first_tasks(t, out):
         def task(r):
@@ -312,7 +347,11 @@
             share = product(gpts + lo) if both else None
             for i in range(step_levels):
                 at = slice(i * LANES, (i + 1) * LANES)
-                following = carry * jnp.exp2(softplus2(depth[:, at]) * rate)
+                depths = softplus2(depth[:, at])
+                if form == 1:
+                    following = carry * power(depths * (rate / 16.0))
+                else:
+                    following = carry * jnp.exp2(depths * rate)
                 term = following
                 if both:
                     term = (carry - following) * softplus2(share[:, at])
@@ -422,7 +461,7 @@
     x = packed.at[which]
     emitted = sweep(
         x, first, bias, second, heads, reach, jnp.ones((gpts, LANES), F32), gpts,
-        -depth_scale, True, buffers, 2 * SUBS if which else SUBS,
+        -depth_scale, True, buffers, 1 - which,
     )
     planck = jnp.exp(0.25 * x[pl.ds(0, levels, stride=SUBS), :])
     out[...] = -(heat_scale * LN2 / gpts) * planck * emitted
@@ -440,12 +479,12 @@
     cosine = jnp.where(cosine > 0.0, cosine, 1.0)
     emitted = sweep(
         work_x, first, bias, second, heads, reach, flux[...], gpts,
-        -depth_scale / cosine, False, buffers, SUBS,
+        -depth_scale / cosine, False, buffers, 0,
     )
     out[...] = (heat_scale / gpts) * cosine[0:1] * emitted
 
 
-def finish_body(me, count, long_first, long_last, work, partner, slot_of, *rest):
+def finish_body(n_group, me, count, long_first, long_last, work, partner, slot_of, *rest):
     pieces, heat = rest[:-1], rest[-1]
     levels, cols = heat.shape
     half = cols // 2
@@ -461,16 +500,20 @@
             far = lane_take(partner[r : r + SUBS, :], place)
             short = jnp.where(lit, jnp.where(here, near, far), 0.0)
             heat[r : r + SUBS, lo : lo + half] = long[r : r + SUBS, :] + short
-    for goal, out in partners(me, pieces):
+    for goal, out in zip(goals(me, n_group), pieces):
         out[...] = heat[pl.ds(pl.multiple_of(goal * slab, SUBS), slab), :]
 
 
-def add_body(me, closed, *rest):
+def add_body(n_group, me, closed, *rest):
     pieces, out = rest[:-1], rest[-1]
     cols = pieces[0].shape[1]
-    for source, piece in partners(me, pieces):
+
+    def place(source, piece):
         at = pl.ds(pl.multiple_of(source * cols, LANES), cols)
         out[:, at] = closed[:, at] + piece[...]
+
+    for source, piece in zip(origins(me, n_group), pieces):
+        pl.when(source >= 0)(functools.partial(place, jnp.maximum(source, 0), piece))
 
 
 def per_device(
@@ -480,7 +523,8 @@
 ):
     n_group = lax.axis_size("group")
     n_tile = lax.axis_size("tile")
-    assert n_group & (n_group - 1) == 0 and n_tile % 2 == 0
+    assert n_tile % 2 == 0
+    n_pieces = 1 + len(rounds(n_group))
     me = lax.axis_index("group").astype(jnp.int32).reshape(1)
     place = lax.axis_index("tile").astype(jnp.int32).reshape(1)
     slab, tile = potential.shape
@@ -499,22 +543,20 @@
     def paired(value):
         return lax.ppermute(value, "tile", [(i, i ^ 1) for i in range(n_tile)])
 
-    def swapped(value, bit):
-        return lax.ppermute(value, "group", [(i, i ^ bit) for i in range(n_group)])
-
     def exchanged(pieces):
-        return [swapped(p, bit) if bit else p for bit, p in zip(far_first(n_group), pieces)]
+        moved = [lax.ppermute(p, "group", list(t.items())) for p, t in zip(pieces[1:], rounds(n_group))]
+        return [pieces[0], *moved]
 
     near = neighbours.shape[0]
     raw = (potential, neighbours, diffusion, species)
     framing, *gas_cuts = call(
-        pack_body,
-        [shaped((slab + 2 * near, tile), F32)] + [shaped((gases, slab, cols), BF16)] * n_group,
+        functools.partial(pack_body, n_group),
+        [shaped((slab + 2 * near, tile), F32)] + [shaped((gases, slab, cols), BF16)] * n_pieces,
         [me, *(pltpu.with_memory_space_constraint(a, pltpu.HBM) for a in raw)],
         [
             pltpu.VMEM(neighbours.shape, jnp.int32),
             pltpu.VMEM(diffusion.shape, F32),
-            pltpu.SemaphoreType.DMA((3 + n_group,)),
+            pltpu.SemaphoreType.DMA((3 + n_pieces,)),
         ],
         where=HBM,
     )
@@ -555,8 +597,8 @@
     )
 
     third, *warm_cuts = call(
-        sections_body,
-        [shaped((slab, tile + 2 * HW), F32)] + [shaped((slab, cols), BF16)] * n_group,
+        functools.partial(sections_body, n_group),
+        [shaped((slab, tile + 2 * HW), F32)] + [shaped((slab, cols), BF16)] * n_pieces,
         [me, place, outer, inner, potential, neighbours, diffusion],
         [pltpu.VMEM((slab, 3 * tile), F32)] * 3
         + [pltpu.VMEM((3, *neighbours.shape), jnp.int32), pltpu.VMEM((3, *diffusion.shape), F32)],
@@ -605,13 +647,15 @@
     partner = paired(work)
     long_last = longwave(1)
     heat_cuts = call(
-        finish_body,
-        [shaped((slab, cols), F32)] * n_group,
+        functools.partial(finish_body, n_group),
+        [shaped((slab, cols), F32)] * n_pieces,
         [me, day_count, long_first, long_last, work, partner, slot_of],
         [pltpu.VMEM((levels, cols), F32)],
     )
     heat_pieces = exchanged(heat_cuts)
-    (evolved,) = call(add_body, [shaped((slab, tile), F32)], [me, closed, *heat_pieces])
+    (evolved,) = call(
+        functools.partial(add_body, n_group), [shaped((slab, tile), F32)], [me, closed, *heat_pieces]
+    )
     return evolved
 
 

time: 292 us -> 311 us (1.065)
  starting transfers between devices: 181 us -> 197 us
  Pallas kernels: 102 us -> 106 us
    ppermute x9 -> x15, starting transfers between devices: 179 us -> 195 us  [exchanged(): lax.ppermute(p, 'group', list(t.items()))]
    pallas_call x10, Pallas kernels: 102 us -> 106 us  [call(): pl.pallas_call(body, out_shape=outs, in_specs=in_specs, out_specs=[VMEM f...]
  transfers between devices with their start and end apart: 13 -> 19, of which waited for: 3 -> 3; matrix products, arithmetic and copies ran while one was open for 0% -> 0% of each run, Pallas kernels for 7% -> 8%
where the time goes in v1:
time: 311 us; the launch traced here: 310 us
  starting transfers between devices  197 us (63%)
  Pallas kernels  106 us (34%)
  waiting for transfers between devices  4.18 us (1%)
    ppermute x15, starting transfers between devices, exchanged(): lax.ppermute(p, 'group', list(t.items()))  195 us
    pallas_call x10, Pallas kernels, call(): pl.pallas_call(body, out_shape=outs, in_specs=in_specs, out_specs=[VMEM f...  106 us
  transfers between devices with their start and end apart: 19, of which 3 were waited for; matrix products, arithmetic and copies ran while one was open for 0% of the time, Pallas kernels for 8%

profile of v1, /device:TPU:4, one launch (start us, length us, event | category | flops | bytes accessed | tf_op | source)
XLA Modules:
  0.0 309.5 jit_solution(15704233991216773564)
XLA Ops:
  0.0 1.1 shard_map.163
  1.2 0.0 copy-start.1
  1.2 0.1 collective-permute-start.1
  1.2 1.5 collective-permute-start
  2.8 0.7 collective-permute-start.2
  3.4 1.3 collective-permute-start.3
  4.7 5.6 %collective-permute-start.4 = (bf16[7,16,256]{2,1,0:T(8,128)(2,1)S(1)}, bf16[7,16,256]{2,1,0:T(8,128)(2,1)S(1)}, u32[]{:S(2)}, u32[]{:S(2)}) collective-permute-start(bf16[7,16,256]{2,1,0:T(8,128)(2,1)S(1)} %get-tuple-element.49), channel_id=1, source_target_pairs={{0,24},{24,0},{1,25},{25,1},{2,26},{26,2},{3,27},{27,3},{4,28},{28... | collective-permute-start | bytes 172040 | tf_op jit(solution)/shard_map/ppermute | solution.py:547
  10.3 0.0 collective-permute-done.1.inner
  10.3 1.8 collective-permute-start.5
  12.2 0.1 collective-permute-start.6
  12.3 0.0 copy-start.3
  12.3 0.0 copy-start.4
  12.3 0.0 copy-start.5
  12.3 0.0 copy-start.7
  12.4 0.0 copy-start.8
  12.4 0.0 copy-start.9
  12.4 0.0 copy-start.11
  12.4 0.0 copy-start.12
  12.4 0.0 copy-start.13
  12.4 0.0 copy-start.14
  12.4 2.7 shard_map.164
  15.2 0.0 copy-start.6
  15.2 0.7 collective-permute-start.7
  15.9 1.3 collective-permute-start.8
  17.2 3.6 %collective-permute-start.9 = (bf16[16,256]{1,0:T(8,128)(2,1)S(1)}, bf16[16,256]{1,0:T(8,128)(2,1)S(1)}, u32[]{:S(2)}, u32[]{:S(2)}) collective-permute-start(bf16[16,256]{1,0:T(8,128)(2,1)S(1)} %get-tuple-element.55), channel_id=1, source_target_pairs={{0,24},{24,0},{1,25},{25,1},{2,26},{26,2},{3,27},{27,3},{4,28},{28... | collective-permute-start | bytes 24584 | tf_op jit(solution)/shard_map/ppermute | solution.py:547
  20.8 2.2 collective-permute-start.10
  23.0 0.9 collective-permute-start.11
  24.6 0.0 copy-start.10
  24.7 0.6 copy-done.10
  25.3 0.5 shard_map.166
  25.7 0.0 collective-permute-done.7.rest_7_
  25.8 1.0 collective-permute-done.11.rest_11_
  26.7 0.5 shard_map.167
  27.2 0.1 collective-permute-start.12
  27.3 12.8 %shard_map.168._.long_first = f32[64,128]{1,0:T(8,128)S(1)} custom-call(f32[2,512,128]{2,1,0:T(8,128)S(1)} %get-tuple-element.61.packed.refs_0_, bf16[64,8]{1,0:T(8,128)(2,1)S(1)} %get-tuple-element.62.first.refs_1_, f32[64,128]{1,0:T(8,128)S(1)} %get-tuple-element.63.bias.refs_2_, bf16[64,64]{1,0:T(8,128)(2,1)S(1)} %get-tuple-element.64.second.refs_3_, ...), custom_call_target="tpu_custom_call" | custom-call | flops 536870912 | bytes 738304 | tf_op jit(solution)/shard_map/pallas_call | solution.py:39
  40.2 79.0 %shard_map.169._.work = f32[64,128]{1,0:T(8,128)S(1)} custom-call(f32[64,128]{1,0:T(8,128)S(1)} %shard_map.168._.long_first, s32[1,1]{1,0:T(1,128)S(6)} %copy.18.refs_0_.count, f32[512,128]{1,0:T(8,128)S(1)} %get-tuple-element.67.refs_1_, f32[8,128]{1,0:T(8,128)S(1)} %get-tuple-element.68.refs_2_, bf16[528,128]{1,0:T(8,128)(2,1)S(1)} %collective-permute-done.12.refs_3_, ...), custom_call_target="tpu_custom_call" | custom-call | flops 234881024 | bytes 689156 | tf_op jit(solution)/shard_map/pallas_call | solution.py:39
  119.1 0.6 collective-permute-start.13
  119.7 8.4 %shard_map.170.long_last = f32[64,128]{1,0:T(8,128)S(1)} custom-call(f32[64,128]{1,0:T(8,128)S(1)} %shard_map.169._.work, f32[2,512,128]{2,1,0:T(8,128)S(1)} %get-tuple-element.61.packed.refs_0_, bf16[64,8]{1,0:T(8,128)(2,1)S(1)} %get-tuple-element.62.first.refs_1_, f32[64,128]{1,0:T(8,128)S(1)} %get-tuple-element.63.bias.refs_2_, ...), custom_call_target="tpu_custom_call" | custom-call | flops 536870912 | bytes 771072 | tf_op jit(solution)/shard_map/pallas_call | solution.py:39
  128.1 0.1 shard_map.171
  128.2 0.7 collective-permute-start.14
  128.9 1.3 collective-permute-start.15
  130.2 173.0 %collective-permute-start.16 = (f32[16,256]{1,0:T(8,128)S(1)}, f32[16,256]{1,0:T(8,128)S(1)}, u32[]{:S(2)}, u32[]{:S(2)}) collective-permute-start(f32[16,256]{1,0:T(8,128)S(1)} %get-tuple-element.80), channel_id=1, source_target_pairs={{0,24},{24,0},{1,25},{25,1},{2,26},{26,2},{3,27},{27,3},{4,28},{28... | collective-permute-start | bytes 49160 | tf_op jit(solution)/shard_map/ppermute | solution.py:547
  303.2 1.8 collective-permute-start.17
  305.1 0.1 collective-permute-start.18
  305.2 0.5 shard_map.165.closed
  305.7 0.8 collective-permute-done.17.rest_4_
  306.5 2.4 collective-permute-done.18.rest_5_
  308.9 0.7 shard_map.172
  (30 shorter events, 0.1 us)
Async XLA Ops:
  0.0 12.3 %copy-start = (f32[16,1024]{1,0:T(8,128)S(1)}, f32[16,1024]{1,0:T(8,128)}, u32[]{:S(2)}) copy-start(f32[16,1024]{1,0:T(8,128)} %own.3) | copy-start | bytes 196612
  0.0 12.3 %copy-start.2 = (f32[4,1024]{1,0:T(4,128)S(1)}, f32[4,1024]{1,0:T(4,128)}, u32[]{:S(2)}) copy-start(f32[4,1024]{1,0:T(4,128)} %weight.5) | copy-start | bytes 49156
  1.2 11.1 %copy-start.1 = (s32[4,1024]{1,0:T(4,128)S(1)}, s32[4,1024]{1,0:T(4,128)}, u32[]{:S(2)}) copy-start(s32[4,1024]{1,0:T(4,128)} %table.5) | copy-start | bytes 49156
  1.2 9.2 %collective-permute-start.1 = (f32[24,1024]{1,0:T(8,128)S(1)}, f32[24,1024]{1,0:T(8,128)S(1)}, u32[]{:S(2)}, u32[]{:S(2)}) collective-permute-start(f32[24,1024]{1,0:T(8,128)S(1)} %get-tuple-element.44._), channel_id=1, source_target_pairs={{0,1},{1,0},{2,3},{3,2},{4,5},{5,4},{6,7},{7,6},{8,9},{9,8},{10,11... | collective-permute-start | bytes 294920 | tf_op jit(solution)/shard_map/ppermute | solution.py:544
  1.2 10.9 %collective-permute-start = (f32[24,1024]{1,0:T(8,128)S(1)}, f32[24,1024]{1,0:T(8,128)S(1)}, u32[]{:S(2)}, u32[]{:S(2)}) collective-permute-start(f32[24,1024]{1,0:T(8,128)S(1)} %get-tuple-element.44._), channel_id=1, source_target_pairs={{0,7},{1,2},{2,1},{3,4},{4,3},{5,6},{6,5},{7,0},{8,15},{9,10},{10,... | collective-permute-start | bytes 294920 | tf_op jit(solution)/shard_map/ppermute | solution.py:541
  2.8 12.4 %collective-permute-start.2 = (bf16[7,16,256]{2,1,0:T(8,128)(2,1)S(1)}, bf16[7,16,256]{2,1,0:T(8,128)(2,1)S(1)}, u32[]{:S(2)}, u32[]{:S(2)}) collective-permute-start(bf16[7,16,256]{2,1,0:T(8,128)(2,1)S(1)} %get-tuple-element.47), channel_id=1, source_target_pairs={{8,16},{16,8},{9,17},{17,9},{10,18},{18,10},{11,19},{19,11},{12,20... | collective-permute-start | bytes 172040 | tf_op jit(solution)/shard_map/ppermute | solution.py:547
  3.4 12.4 %collective-permute-start.3 = (bf16[7,16,256]{2,1,0:T(8,128)(2,1)S(1)}, bf16[7,16,256]{2,1,0:T(8,128)(2,1)S(1)}, u32[]{:S(2)}, u32[]{:S(2)}) collective-permute-start(bf16[7,16,256]{2,1,0:T(8,128)(2,1)S(1)} %get-tuple-element.48), channel_id=1, source_target_pairs={{16,0},{8,24},{17,1},{9,25},{18,2},{10,26},{19,3},{11,27},{20,4},{... | collective-permute-start | bytes 172040 | tf_op jit(solution)/shard_map/ppermute | solution.py:547
  4.7 12.4 %collective-permute-start.4 = (bf16[7,16,256]{2,1,0:T(8,128)(2,1)S(1)}, bf16[7,16,256]{2,1,0:T(8,128)(2,1)S(1)}, u32[]{:S(2)}, u32[]{:S(2)}) collective-permute-start(bf16[7,16,256]{2,1,0:T(8,128)(2,1)S(1)} %get-tuple-element.49), channel_id=1, source_target_pairs={{0,24},{24,0},{1,25},{25,1},{2,26},{26,2},{3,27},{27,3},{4,28},{28... | collective-permute-start | bytes 172040 | tf_op jit(solution)/shard_map/ppermute | solution.py:547
  10.3 10.5 %collective-permute-start.5 = (bf16[7,16,256]{2,1,0:T(8,128)(2,1)S(1)}, bf16[7,16,256]{2,1,0:T(8,128)(2,1)S(1)}, u32[]{:S(2)}, u32[]{:S(2)}) collective-permute-start(bf16[7,16,256]{2,1,0:T(8,128)(2,1)S(1)} %get-tuple-element.50), channel_id=1, source_target_pairs={{24,16},{0,8},{25,17},{1,9},{26,18},{2,10},{27,19},{3,11},{28,20},... | collective-permute-start | bytes 172040 | tf_op jit(solution)/shard_map/ppermute | solution.py:547
  12.2 10.8 %collective-permute-start.6 = (bf16[7,16,256]{2,1,0:T(8,128)(2,1)S(1)}, bf16[7,16,256]{2,1,0:T(8,128)(2,1)S(1)}, u32[]{:S(2)}, u32[]{:S(2)}) collective-permute-start(bf16[7,16,256]{2,1,0:T(8,128)(2,1)S(1)} %get-tuple-element.51), channel_id=1, source_target_pairs={{24,8},{8,0},{0,16},{16,24},{25,9},{9,1},{1,17},{17,25},{26,10},{1... | collective-permute-start | bytes 172040 | tf_op jit(solution)/shard_map/ppermute | solution.py:547
  12.3 12.3 %copy-start.3 = (bf16[64,256]{1,0:T(8,128)(2,1)S(1)}, bf16[64,256]{1,0:T(8,128)(2,1)}, u32[]{:S(2)}) copy-start(bf16[64,256]{1,0:T(8,128)(2,1)} %refs_6_.1) | copy-start | bytes 98308
  12.3 12.3 %copy-start.4 = (bf16[64,256]{1,0:T(8,128)(2,1)S(1)}, bf16[64,256]{1,0:T(8,128)(2,1)}, u32[]{:S(2)}) copy-start(bf16[64,256]{1,0:T(8,128)(2,1)} %refs_7_.1) | copy-start | bytes 98308
  12.3 12.3 %copy-start.5 = (bf16[64,224]{1,0:T(8,128)(2,1)S(1)}, bf16[64,224]{1,0:T(8,128)(2,1)}, u32[]{:S(2)}) copy-start(bf16[64,224]{1,0:T(8,128)(2,1)} %refs_11_.1) | copy-start | bytes 86020
  12.3 12.3 %copy-start.7 = (bf16[64,64]{1,0:T(8,128)(2,1)S(1)}, bf16[64,64]{1,0:T(8,128)(2,1)}, u32[]{:S(2)}) copy-start(bf16[64,64]{1,0:T(8,128)(2,1)} %refs_10_.1) | copy-start | bytes 24580
  12.4 12.3 %copy-start.8 = (bf16[8,64]{1,0:T(8,128)(2,1)S(1)}, bf16[8,64]{1,0:T(8,128)(2,1)}, u32[]{:S(2)}) copy-start(bf16[8,64]{1,0:T(8,128)(2,1)} %refs_3_.1) | copy-start | bytes 3076
  12.4 12.3 %copy-start.9 = (bf16[8,64]{1,0:T(8,128)(2,1)S(1)}, bf16[8,64]{1,0:T(8,128)(2,1)}, u32[]{:S(2)}) copy-start(bf16[8,64]{1,0:T(8,128)(2,1)} %refs_8_.1) | copy-start | bytes 3076
  12.4 12.3 %copy-start.11 = (bf16[1,1,256]{2,1,0:T(2,128)(2,1)S(1)}, bf16[1,1,256]{2,1,0:T(2,128)(2,1)}, u32[]{:S(2)}) copy-start(bf16[1,1,256]{2,1,0:T(2,128)(2,1)} %refs_2_.1) | copy-start | bytes 1540
  12.4 12.3 %copy-start.12 = (f32[224]{0:T(256)S(1)}, f32[224]{0:T(256)}, u32[]{:S(2)}) copy-start(f32[224]{0:T(256)} %param.33) | copy-start | bytes 2692
  12.4 12.3 %copy-start.13 = (f32[64]{0:T(128)S(1)}, f32[64]{0:T(128)}, u32[]{:S(2)}) copy-start(f32[64]{0:T(128)} %param.25) | copy-start | bytes 772
  12.4 12.3 %copy-start.14 = (f32[64]{0:T(128)S(1)}, f32[64]{0:T(128)}, u32[]{:S(2)}) copy-start(f32[64]{0:T(128)} %param.30) | copy-start | bytes 772
  15.2 9.5 %copy-start.6 = (bf16[64,64]{1,0:T(8,128)(2,1)S(1)}, bf16[64,64]{1,0:T(8,128)(2,1)}, u32[]{:S(2)}) copy-start(bf16[64,64]{1,0:T(8,128)(2,1)} %refs_5_.1) | copy-start | bytes 24580
  15.2 10.5 %collective-permute-start.7 = (bf16[16,256]{1,0:T(8,128)(2,1)S(1)}, bf16[16,256]{1,0:T(8,128)(2,1)S(1)}, u32[]{:S(2)}, u32[]{:S(2)}) collective-permute-start(bf16[16,256]{1,0:T(8,128)(2,1)S(1)} %get-tuple-element.53), channel_id=1, source_target_pairs={{8,16},{16,8},{9,17},{17,9},{10,18},{18,10},{11,19},{19,11},{12,20... | collective-permute-start | bytes 24584 | tf_op jit(solution)/shard_map/ppermute | solution.py:547
  15.9 9.9 %collective-permute-start.8 = (bf16[16,256]{1,0:T(8,128)(2,1)S(1)}, bf16[16,256]{1,0:T(8,128)(2,1)S(1)}, u32[]{:S(2)}, u32[]{:S(2)}) collective-permute-start(bf16[16,256]{1,0:T(8,128)(2,1)S(1)} %get-tuple-element.54), channel_id=1, source_target_pairs={{16,0},{8,24},{17,1},{9,25},{18,2},{10,26},{19,3},{11,27},{20,4},{... | collective-permute-start | bytes 24584 | tf_op jit(solution)/shard_map/ppermute | solution.py:547
  17.2 8.6 %collective-permute-start.9 = (bf16[16,256]{1,0:T(8,128)(2,1)S(1)}, bf16[16,256]{1,0:T(8,128)(2,1)S(1)}, u32[]{:S(2)}, u32[]{:S(2)}) collective-permute-start(bf16[16,256]{1,0:T(8,128)(2,1)S(1)} %get-tuple-element.55), channel_id=1, source_target_pairs={{0,24},{24,0},{1,25},{25,1},{2,26},{26,2},{3,27},{27,3},{4,28},{28... | collective-permute-start | bytes 24584 | tf_op jit(solution)/shard_map/ppermute | solution.py:547
  20.8 4.9 %collective-permute-start.10 = (bf16[16,256]{1,0:T(8,128)(2,1)S(1)}, bf16[16,256]{1,0:T(8,128)(2,1)S(1)}, u32[]{:S(2)}, u32[]{:S(2)}) collective-permute-start(bf16[16,256]{1,0:T(8,128)(2,1)S(1)} %get-tuple-element.56), channel_id=1, source_target_pairs={{24,16},{0,8},{25,17},{1,9},{26,18},{2,10},{27,19},{3,11},{28,20},... | collective-permute-start | bytes 24584 | tf_op jit(solution)/shard_map/ppermute | solution.py:547
  23.0 3.7 %collective-permute-start.11 = (bf16[16,256]{1,0:T(8,128)(2,1)S(1)}, bf16[16,256]{1,0:T(8,128)(2,1)S(1)}, u32[]{:S(2)}, u32[]{:S(2)}) collective-permute-start(bf16[16,256]{1,0:T(8,128)(2,1)S(1)} %get-tuple-element.57), channel_id=1, source_target_pairs={{24,8},{8,0},{0,16},{16,24},{25,9},{9,1},{1,17},{17,25},{26,10},{1... | collective-permute-start | bytes 24584 | tf_op jit(solution)/shard_map/ppermute | solution.py:547
  24.6 0.7 copy-start.10
  27.2 12.9 %collective-permute-start.12 = (bf16[528,128]{1,0:T(8,128)(2,1)S(1)}, bf16[528,128]{1,0:T(8,128)(2,1)S(1)}, u32[]{:S(2)}, u32[]{:S(2)}) collective-permute-start(bf16[528,128]{1,0:T(8,128)(2,1)S(1)} %get-tuple-element.69), channel_id=1, source_target_pairs={{0,1},{1,0},{2,3},{3,2},{4,5},{5,4},{6,7},{7,6},{8,9},{9,8},{10,11... | collective-permute-start | bytes 405512 | tf_op jit(solution)/shard_map/ppermute | solution.py:544
  119.1 9.0 %collective-permute-start.13 = (f32[64,128]{1,0:T(8,128)S(1)}, f32[64,128]{1,0:T(8,128)S(1)}, u32[]{:S(2)}, u32[]{:S(2)}) collective-permute-start(f32[64,128]{1,0:T(8,128)S(1)} %shard_map.169._.work), channel_id=1, source_target_pairs={{0,1},{1,0},{2,3},{3,2},{4,5},{5,4},{6,7},{7,6},{8,9},{9,8},{10,11... | collective-permute-start | bytes 98312 | tf_op jit(solution)/shard_map/ppermute | solution.py:544
  128.2 177.4 %collective-permute-start.14 = (f32[16,256]{1,0:T(8,128)S(1)}, f32[16,256]{1,0:T(8,128)S(1)}, u32[]{:S(2)}, u32[]{:S(2)}) collective-permute-start(f32[16,256]{1,0:T(8,128)S(1)} %get-tuple-element.78), channel_id=1, source_target_pairs={{8,16},{16,8},{9,17},{17,9},{10,18},{18,10},{11,19},{19,11},{12,20... | collective-permute-start | bytes 49160 | tf_op jit(solution)/shard_map/ppermute | solution.py:547
  128.9 176.8 %collective-permute-start.15 = (f32[16,256]{1,0:T(8,128)S(1)}, f32[16,256]{1,0:T(8,128)S(1)}, u32[]{:S(2)}, u32[]{:S(2)}) collective-permute-start(f32[16,256]{1,0:T(8,128)S(1)} %get-tuple-element.79), channel_id=1, source_target_pairs={{16,0},{8,24},{17,1},{9,25},{18,2},{10,26},{19,3},{11,27},{20,4},{... | collective-permute-start | bytes 49160 | tf_op jit(solution)/shard_map/ppermute | solution.py:547
  130.2 175.5 %collective-permute-start.16 = (f32[16,256]{1,0:T(8,128)S(1)}, f32[16,256]{1,0:T(8,128)S(1)}, u32[]{:S(2)}, u32[]{:S(2)}) collective-permute-start(f32[16,256]{1,0:T(8,128)S(1)} %get-tuple-element.80), channel_id=1, source_target_pairs={{0,24},{24,0},{1,25},{25,1},{2,26},{26,2},{3,27},{27,3},{4,28},{28... | collective-permute-start | bytes 49160 | tf_op jit(solution)/shard_map/ppermute | solution.py:547
  303.2 3.3 %collective-permute-start.17 = (f32[16,256]{1,0:T(8,128)S(1)}, f32[16,256]{1,0:T(8,128)S(1)}, u32[]{:S(2)}, u32[]{:S(2)}) collective-permute-start(f32[16,256]{1,0:T(8,128)S(1)} %get-tuple-element.81), channel_id=1, source_target_pairs={{24,16},{0,8},{25,17},{1,9},{26,18},{2,10},{27,19},{3,11},{28,20},... | collective-permute-start | bytes 49160 | tf_op jit(solution)/shard_map/ppermute | solution.py:547
  305.1 3.8 %collective-permute-start.18 = (f32[16,256]{1,0:T(8,128)S(1)}, f32[16,256]{1,0:T(8,128)S(1)}, u32[]{:S(2)}, u32[]{:S(2)}) collective-permute-start(f32[16,256]{1,0:T(8,128)S(1)} %get-tuple-element.82), channel_id=1, source_target_pairs={{24,8},{8,0},{0,16},{16,24},{25,9},{9,1},{1,17},{17,25},{26,10},{1... | collective-permute-start | bytes 49160 | tf_op jit(solution)/shard_map/ppermute | solution.py:547
